TPU v7x, 32 devices: a whole 2x2x4 slice. The times are simulated.
32 devices in a mesh: dom: 16 (over z, x, core), band: 2 (over y).
Axes of the slice: x: 2, y: 2, z: 4, core: 2. Of those that a mesh axis runs over, the one named last changes fastest.
Arguments:
- ensemble: float32 [16, 3, 32, 4096], P('dom', None, 'band'), may hold values from -6 to 6
- ancestors: int32 [16], P('dom'), may hold values from 0 to 15
- sea_depth: float32 [32, 4096], P('band'), may hold values from 1 to 2
- obs_rows: int32 [4096], P('band'), may hold values from 0 to 31, as said below
- obs_cols: int32 [4096], P('band'), may hold values from 0 to 4095
- obs_values: float32 [4096], P('band'), may hold values from -6 to 6
Outputs:
- forecast: float32 [16, 3, 32, 4096], P('dom', None, 'band')
Inputs may be any that keep to these rules, and one draw needn't show every extreme that they name: `obs_rows`: observations b * 2048 to (b + 1) * 2048 - 1 lie in rows b * 16 to (b + 1) * 16 - 1; no two observations share a cell.
All inputs are finite; a program needn't handle non-finite values.
Results may differ from a plain program's by a relative error of at most 0.00016.
Values sent between devices are 32-bit elements; how exact they have to be, the bound alone decides.
A program may use at most 64 MiB of HBM per device.

v0:
```python
import jax
import jax.numpy as jnp
from jax import lax
from jax.sharding import PartitionSpec as P

STEPS = 4
BW = 8


TIME_STEP = 0.8
NUDGE_GAIN = 0.5
LENGTH_SCALE = 3.0


def extended(cells, sides, width):
    for axis, dim in sides:
        count = lax.axis_size(axis)
        ends = count - 1
        head = lax.slice_in_dim(cells, 0, width, axis=dim)
        tail = lax.slice_in_dim(cells, cells.shape[dim] - width, cells.shape[dim], axis=dim)
        cells = jnp.concatenate(
            [
                lax.ppermute(tail, axis, [(i, (i + 1) % count) for i in range(ends)]),
                cells,
                lax.ppermute(head, axis, [((i + 1) % count, i) for i in range(ends)]),
            ],
            axis=dim,
        )
    return cells


def kernel(offset):
    distance = jnp.abs(offset).astype(jnp.float32)
    return jnp.where(distance <= BW, jnp.exp(-distance / LENGTH_SCALE), jnp.float32(0.0))


def advance(height, east_vel, north_vel, sea_depth, coriolis, inside):
    flux_east = sea_depth * east_vel
    flux_north = sea_depth * north_vel
    east_diff = 0.5 * (jnp.roll(flux_east, -1, -1) - jnp.roll(flux_east, 1, -1))[:, 1:-1]
    north_diff = 0.5 * (flux_north[:, 2:] - flux_north[:, :-2])
    new_height = jnp.where(
        inside[1:-1, None], height[:, 1:-1] - TIME_STEP * (east_diff + north_diff), jnp.float32(0.0)
    )
    slope_east = 0.5 * (jnp.roll(new_height, -1, -1) - jnp.roll(new_height, 1, -1))[:, 1:-1]
    slope_north = 0.5 * (new_height[:, 2:] - new_height[:, :-2])
    turning = coriolis[2:-2, None]
    keeping = inside[2:-2, None]
    new_east = jnp.where(
        keeping,
        east_vel[:, 2:-2] + TIME_STEP * (turning * north_vel[:, 2:-2] - slope_east),
        jnp.float32(0.0),
    )
    new_north = jnp.where(
        keeping,
        north_vel[:, 2:-2] + TIME_STEP * (-turning * east_vel[:, 2:-2] - slope_north),
        jnp.float32(0.0),
    )
    return (new_height[:, 1:-1], new_east, new_north)


def on_device(ensemble, ancestors, sea_depth, obs_rows, obs_cols, obs_values):
    local_count, fields, band_rows, columns = ensemble.shape
    lineage = lax.all_gather(ancestors, "dom", axis=0, tiled=True)
    crossed = lax.all_to_all(ensemble, "dom", split_axis=3, concat_axis=0, tiled=True)
    chosen = jnp.take(crossed, lineage, axis=0)
    state = lax.all_to_all(chosen, "dom", split_axis=0, concat_axis=3, tiled=True)
    band_start = lax.axis_index("band") * band_rows
    local_rows = obs_rows - band_start
    position = local_rows * columns + obs_cols
    height = state[:, 0]
    east_vel = state[:, 1]
    north_vel = state[:, 2]
    sampled = jnp.take(height.reshape(local_count, band_rows * columns), position, axis=1)
    innovation = obs_values[None, :] - sampled
    col_index = jnp.arange(columns)
    placing = (local_rows[:, None] == jnp.arange(band_rows)[None, :]).astype(jnp.float32)
    picked_rows = kernel(obs_cols[:, None] - col_index[None, :])
    weighted = innovation[:, :, None] * picked_rows[None]
    spread_field = jnp.einsum("or,poc->prc", placing, weighted, precision=lax.Precision.HIGHEST)
    widened = extended(spread_field, (("band", 1),), BW)
    row_kernel = kernel(
        jnp.arange(band_rows)[:, None] - jnp.arange(band_rows + 2 * BW)[None, :] + BW
    )
    increment = jnp.einsum("rm,pmc->prc", row_kernel, widened, precision=lax.Precision.HIGHEST)
    height = height + NUDGE_GAIN * increment
    margin = 2 * STEPS
    total_rows = band_rows * lax.axis_size("band")
    depth_wide = extended(sea_depth, (("band", 0),), margin)
    global_rows = band_start - margin + jnp.arange(band_rows + 2 * margin)
    inside_all = (global_rows >= 0) & (global_rows < total_rows)
    coriolis_all = 0.1 + 0.4 * ((global_rows.astype(jnp.float32) + 0.5) / total_rows)
    first_row = margin - 2
    last_row = first_row + band_rows + 4
    for section_no in range(STEPS):
        stacked = jnp.stack([height, east_vel, north_vel], axis=1)
        widened_state = extended(stacked, (("band", 2),), 2)
        height, east_vel, north_vel = advance(
            widened_state[:, 0],
            widened_state[:, 1],
            widened_state[:, 2],
            depth_wide[first_row:last_row],
            coriolis_all[first_row:last_row],
            inside_all[first_row:last_row],
        )
    return jnp.stack([height, east_vel, north_vel], axis=1)


def solution(mesh):
    placed = (
        P("dom", None, "band", None),
        P("dom"),
        P("band", None),
        P("band"),
        P("band"),
        P("band"),
    )
    return jax.shard_map(
        on_device,
        mesh=mesh,
        in_specs=placed,
        out_specs=P("dom", None, "band", None),
        check_vma=False,
    )
```

profile of v0, /device:TPU:12, one launch (start us, length us, event | category | flops | bytes accessed | tf_op | source)
XLA Modules:
  0.0 171.9 jit_solution(9957151525892860108)
XLA Ops:
  0.0 6.9 %copy.10 = f32[1,3,16,4096]{2,1,0,3:T(4,128)} copy(f32[1,3,16,4096]{3,2,1,0:T(8,128)} %param.6) | data formatting | bytes 1572864 | tf_op args[0]
  6.9 9.1 %reshape.516 = f32[16,1,12288]{2,1,0:T(1,128)} reshape(f32[4096,1,3,16]{3,2,1,0:T(4,128)} %bitcast.132) | data formatting | bytes 1572864
  16.0 6.4 %all-to-all-start = ((f32[16,1,12288]{2,1,0:T(1,128)}), f32[16,1,12288]{2,1,0:T(1,128)S(1)}, u32[]{:S(2)}, u32[]{:S(2)}) async-start(f32[16,1,12288]{2,1,0:T(1,128)} %reshape.516), calls=%async_computation | async-start | bytes 1572864 | tf_op jit(solution)/shard_map/all_to_all | solution.py:65
  23.1 0.6 dynamic-slice
  23.7 0.7 dynamic-update-slice
  24.4 15.9 %all-reduce = s32[16]{0:T(128)S(1)} all-reduce(s32[16]{0:T(128)S(1)} %dynamic-update-slice), channel_id=1, replica_groups=mesh['dom'=16,'band'=2] {'dom'}, use_global_device_ids=true, to_apply=%add | all-reduce | flops 16 | bytes 128
  40.3 1.1 all-to-all-done
  41.4 0.5 broadcast.98
  41.9 2.5 %reduce = f32[16,12288]{1,0:T(8,128)S(1)} reduce(f32[16,1,12288]{2,1,0:T(1,128)S(1)} %all-to-all-done, f32[]{:T(128)} %broadcast.98), dimensions={1}, to_apply=%all_to_all.26.reduce_sub_computation | reduce | bytes 1572868 | tf_op jit(solution)/shard_map/all_to_all | solution.py:65
  44.5 7.5 %reshape.517 = f32[4096,1,3,16]{3,2,1,0:T(4,128)} reshape(f32[16,12288]{1,0:T(8,128)S(1)} %reduce) | data formatting | bytes 1572864
  52.0 6.4 %copy.12 = f32[1,3,16,16,256]{4,2,1,3,0:T(8,128)S(1)} copy(f32[1,3,16,16,256]{2,1,4,3,0:T(4,128)} %bitcast.131) | data formatting | bytes 1572864 | tf_op jit(solution)/shard_map/all_to_all | solution.py:65
  58.4 0.6 gather_fusion
  59.0 1.0 broadcast_select_fusion
  60.0 6.0 %all-to-all-start.1 = ((f32[16,3,16,256]{3,2,1,0:T(8,128)}), f32[16,3,16,256]{3,2,1,0:T(8,128)S(1)}, u32[]{:S(2)}, u32[]{:S(2)}) async-start(f32[16,3,16,256]{3,2,1,0:T(8,128)} %broadcast_select_fusion), calls=%async_computation.1 | async-start | bytes 1572864 | tf_op jit(solution)/shard_map/all_to_all | solution.py:67
  66.0 2.4 %collective-permute-start.5 = (f32[8,4096]{1,0:T(8,128)S(1)}, f32[8,4096]{1,0:T(8,128)S(1)}, u32[]{:S(2)}, u32[]{:S(2)}) collective-permute-start(f32[8,4096]{1,0:T(8,128)S(1)} %get-tuple-element.80), channel_id=1, source_target_pairs={{1,0},{3,2},{5,4},{7,6},{9,8},{11,10},{13,12},{15,14},{17,16},{19,... | collective-permute-start | bytes 393224 | tf_op jit(solution)/shard_map/ppermute | solution.py:25
  68.4 1.3 collective-permute-start.4
  69.8 15.1 %all-to-all-done.1 = f32[16,3,16,256]{3,2,1,0:T(8,128)S(1)} async-done(((f32[16,3,16,256]{3,2,1,0:T(8,128)}), f32[16,3,16,256]{3,2,1,0:T(8,128)S(1)}, u32[]{:S(2)}, u32[]{:S(2)}) %all-to-all-start.1) | async-done | bytes 786464 | tf_op jit(solution)/shard_map/all_to_all | solution.py:67
  85.1 11.8 %gather_fusion.1 = f32[2048]{0:T(1024)S(1)} fusion(f32[65536]{0:T(1024)S(1)} %bitcast.130, s32[2048]{0:T(1024)S(1)} %get-tuple-element.7), kind=kCustom, calls=%fused_computation.1 | custom fusion | bytes 24576 | tf_op jit(solution)/shard_map/jit(_take)/gather | solution.py:74
  96.9 25.4 %fusion.15 = f32[1,16,4096]{2,1,0:T(8,128)S(1)} fusion(s32[2048]{0:T(1024)S(1)} %copy-done.1, f32[2048]{0:T(1024)S(1)} %select_subtract_fusion, s32[2048]{0:T(1024)S(1)} %get-tuple-element.8), kind=kOutput, calls=%fused_computation.18 | convolution fusion | flops 1677754368 | bytes 286720 | tf_op jit(solution)/shard_map/or,poc->prc/dot_general | solution.py:80
  122.4 2.4 %collective-permute-start.1 = (f32[1,8,4096]{2,1,0:T(8,128)S(1)}, f32[1,8,4096]{2,1,0:T(8,128)S(1)}, u32[]{:S(2)}, u32[]{:S(2)}) collective-permute-start(f32[1,8,4096]{2,1,0:T(8,128)S(1)} %get-tuple-element.82), channel_id=1, source_target_pairs={{1,0},{3,2},{5,4},{7,6},{9,8},{11,10},{13,12},{15,14},{17,16},{19,... | collective-permute-start | bytes 393224 | tf_op jit(solution)/shard_map/ppermute | solution.py:25
  124.8 1.3 collective-permute-start
  126.2 2.3 %collective-permute-done.1 = f32[1,8,4096]{2,1,0:T(8,128)S(1)} collective-permute-done((f32[1,8,4096]{2,1,0:T(8,128)S(1)}, f32[1,8,4096]{2,1,0:T(8,128)S(1)}, u32[]{:S(2)}, u32[]{:S(2)}) %collective-permute-start.1) | collective-permute-done | bytes 131104 | tf_op jit(solution)/shard_map/ppermute | solution.py:25
  128.4 4.1 %collective-permute-done = f32[1,8,4096]{2,1,0:T(8,128)S(1)} collective-permute-done((f32[1,8,4096]{2,1,0:T(8,128)S(1)}, f32[1,8,4096]{2,1,0:T(8,128)S(1)}, u32[]{:S(2)}, u32[]{:S(2)}) %collective-permute-start) | collective-permute-done | bytes 131104 | tf_op jit(solution)/shard_map/ppermute | solution.py:23
  132.6 0.4 fusion.20
  133.1 1.5 collective-permute-start.3
  134.5 1.5 collective-permute-start.2
  136.2 0.5 collective-permute-done.3
  136.7 4.3 %collective-permute-done.2 = f32[1,3,2,4096]{3,2,1,0:T(2,128)S(1)} collective-permute-done((f32[1,3,2,4096]{3,2,1,0:T(2,128)S(1)}, f32[1,3,2,4096]{3,2,1,0:T(2,128)S(1)}, u32[]{:S(2)}, u32[]{:S(2)}) %collective-permute-start.2) | collective-permute-done | bytes 98336 | tf_op jit(solution)/shard_map/ppermute | solution.py:23
  141.0 0.2 pad_maximum_fusion
  141.4 0.2 fusion.143
  141.7 0.2 fusion.44
  142.0 0.2 fusion.141
  142.2 0.3 fusion.105
  142.6 1.5 collective-permute-start.7
  144.1 1.3 collective-permute-start.6
  145.4 0.9 collective-permute-done.7
  146.3 4.3 %collective-permute-done.6 = f32[1,3,2,4096]{3,2,1,0:T(2,128)S(1)} collective-permute-done((f32[1,3,2,4096]{3,2,1,0:T(2,128)S(1)}, f32[1,3,2,4096]{3,2,1,0:T(2,128)S(1)}, u32[]{:S(2)}, u32[]{:S(2)}) %collective-permute-start.6) | collective-permute-done | bytes 98336 | tf_op jit(solution)/shard_map/ppermute | solution.py:23
  150.6 0.2 pad_maximum_fusion.1
  150.8 0.1 fusion.51
  150.9 0.2 fusion.139
  151.2 0.2 fusion.39
  151.5 0.2 fusion.137
  151.7 0.3 fusion.92
  152.1 1.5 collective-permute-start.9
  153.6 1.3 collective-permute-start.8
  154.9 0.9 collective-permute-done.9
  155.8 4.3 %collective-permute-done.8 = f32[1,3,2,4096]{3,2,1,0:T(2,128)S(1)} collective-permute-done((f32[1,3,2,4096]{3,2,1,0:T(2,128)S(1)}, f32[1,3,2,4096]{3,2,1,0:T(2,128)S(1)}, u32[]{:S(2)}, u32[]{:S(2)}) %collective-permute-start.8) | collective-permute-done | bytes 98336 | tf_op jit(solution)/shard_map/ppermute | solution.py:23
  160.1 0.2 pad_maximum_fusion.2
  160.3 0.1 fusion.49
  160.5 0.2 fusion.135
  160.7 0.2 fusion.34
  161.0 0.2 fusion.133
  161.2 0.3 fusion.79
  161.6 1.5 collective-permute-start.11
  163.1 1.3 collective-permute-start.10
  164.4 0.9 collective-permute-done.11
  165.3 4.3 %collective-permute-done.10 = f32[1,3,2,4096]{3,2,1,0:T(2,128)S(1)} collective-permute-done((f32[1,3,2,4096]{3,2,1,0:T(2,128)S(1)}, f32[1,3,2,4096]{3,2,1,0:T(2,128)S(1)}, u32[]{:S(2)}, u32[]{:S(2)}) %collective-permute-start.10) | collective-permute-done | bytes 98336 | tf_op jit(solution)/shard_map/ppermute | solution.py:23
  169.6 0.2 pad_maximum_fusion.3
  169.8 0.1 fusion.47
  170.0 0.2 fusion.131
  170.2 0.2 fusion.29
  170.6 0.2 fusion.129
  170.7 0.3 fusion.66
  171.0 0.9 pad_maximum_fusion.4
  (47 shorter events, 1.9 us)
Async XLA Ops:
  16.0 7.1 %copy-start.4 = (u32[32]{0:T(128)S(1)}, u32[32]{0:T(128)}, u32[]{:S(2)}) copy-start(u32[32]{0:T(128)} %constant.78) | copy-start | bytes 388
  16.0 25.4 %all-to-all-start = ((f32[16,1,12288]{2,1,0:T(1,128)}), f32[16,1,12288]{2,1,0:T(1,128)S(1)}, u32[]{:S(2)}, u32[]{:S(2)}) async-start(f32[16,1,12288]{2,1,0:T(1,128)} %reshape.516), calls=%async_computation | async-start | bytes 1572864 | tf_op jit(solution)/shard_map/all_to_all | solution.py:65
  60.0 6.0 %copy-start = (f32[16,4096]{1,0:T(8,128)S(1)}, f32[16,4096]{1,0:T(8,128)}, u32[]{:S(2)}) copy-start(f32[16,4096]{1,0:T(8,128)} %param.8) | copy-start | bytes 786436
  60.0 9.8 %copy-start.1 = (s32[2048]{0:T(1024)S(1)}, s32[2048]{0:T(1024)}, u32[]{:S(2)}) copy-start(s32[2048]{0:T(1024)} %param.10) | copy-start | bytes 24580
  60.0 9.8 %copy-start.3 = (s32[2048]{0:T(1024)S(1)}, s32[2048]{0:T(1024)}, u32[]{:S(2)}) copy-start(s32[2048]{0:T(1024)} %param.9) | copy-start | bytes 24580
  60.0 24.9 %all-to-all-start.1 = ((f32[16,3,16,256]{3,2,1,0:T(8,128)}), f32[16,3,16,256]{3,2,1,0:T(8,128)S(1)}, u32[]{:S(2)}, u32[]{:S(2)}) async-start(f32[16,3,16,256]{3,2,1,0:T(8,128)} %broadcast_select_fusion), calls=%async_computation.1 | async-start | bytes 1572864 | tf_op jit(solution)/shard_map/all_to_all | solution.py:67
  66.0 75.2 %collective-permute-start.5 = (f32[8,4096]{1,0:T(8,128)S(1)}, f32[8,4096]{1,0:T(8,128)S(1)}, u32[]{:S(2)}, u32[]{:S(2)}) collective-permute-start(f32[8,4096]{1,0:T(8,128)S(1)} %get-tuple-element.80), channel_id=1, source_target_pairs={{1,0},{3,2},{5,4},{7,6},{9,8},{11,10},{13,12},{15,14},{17,16},{19,... | collective-permute-start | bytes 393224 | tf_op jit(solution)/shard_map/ppermute | solution.py:25
  68.4 72.8 %collective-permute-start.4 = (f32[8,4096]{1,0:T(8,128)S(1)}, f32[8,4096]{1,0:T(8,128)S(1)}, u32[]{:S(2)}, u32[]{:S(2)}) collective-permute-start(f32[8,4096]{1,0:T(8,128)S(1)} %get-tuple-element.79), channel_id=1, source_target_pairs={{0,1},{2,3},{4,5},{6,7},{8,9},{10,11},{12,13},{14,15},{16,17},{18,... | collective-permute-start | bytes 393224 | tf_op jit(solution)/shard_map/ppermute | solution.py:23
  85.1 11.8 %copy-start.2 = (f32[2048]{0:T(1024)S(1)}, f32[2048]{0:T(1024)}, u32[]{:S(2)}) copy-start(f32[2048]{0:T(1024)} %param.11) | copy-start | bytes 24580
  122.4 6.1 %collective-permute-start.1 = (f32[1,8,4096]{2,1,0:T(8,128)S(1)}, f32[1,8,4096]{2,1,0:T(8,128)S(1)}, u32[]{:S(2)}, u32[]{:S(2)}) collective-permute-start(f32[1,8,4096]{2,1,0:T(8,128)S(1)} %get-tuple-element.82), channel_id=1, source_target_pairs={{1,0},{3,2},{5,4},{7,6},{9,8},{11,10},{13,12},{15,14},{17,16},{19,... | collective-permute-start | bytes 393224 | tf_op jit(solution)/shard_map/ppermute | solution.py:25
  124.8 7.8 %collective-permute-start = (f32[1,8,4096]{2,1,0:T(8,128)S(1)}, f32[1,8,4096]{2,1,0:T(8,128)S(1)}, u32[]{:S(2)}, u32[]{:S(2)}) collective-permute-start(f32[1,8,4096]{2,1,0:T(8,128)S(1)} %get-tuple-element.81), channel_id=1, source_target_pairs={{0,1},{2,3},{4,5},{6,7},{8,9},{10,11},{12,13},{14,15},{16,17},{18,... | collective-permute-start | bytes 393224 | tf_op jit(solution)/shard_map/ppermute | solution.py:23
  133.1 3.7 %collective-permute-start.3 = (f32[1,3,2,4096]{3,2,1,0:T(2,128)S(1)}, f32[1,3,2,4096]{3,2,1,0:T(2,128)S(1)}, u32[]{:S(2)}, u32[]{:S(2)}) collective-permute-start(f32[1,3,2,4096]{3,2,1,0:T(2,128)S(1)} %get-tuple-element.42), channel_id=1, source_target_pairs={{1,0},{3,2},{5,4},{7,6},{9,8},{11,10},{13,12},{15,14},{17,16},{19,... | collective-permute-start | bytes 294920 | tf_op jit(solution)/shard_map/ppermute | solution.py:25
  134.5 6.5 %collective-permute-start.2 = (f32[1,3,2,4096]{3,2,1,0:T(2,128)S(1)}, f32[1,3,2,4096]{3,2,1,0:T(2,128)S(1)}, u32[]{:S(2)}, u32[]{:S(2)}) collective-permute-start(f32[1,3,2,4096]{3,2,1,0:T(2,128)S(1)} %get-tuple-element.41), channel_id=1, source_target_pairs={{0,1},{2,3},{4,5},{6,7},{8,9},{10,11},{12,13},{14,15},{16,17},{18,... | collective-permute-start | bytes 294920 | tf_op jit(solution)/shard_map/ppermute | solution.py:23
  142.6 3.7 %collective-permute-start.7 = (f32[1,3,2,4096]{3,2,1,0:T(2,128)S(1)}, f32[1,3,2,4096]{3,2,1,0:T(2,128)S(1)}, u32[]{:S(2)}, u32[]{:S(2)}) collective-permute-start(f32[1,3,2,4096]{3,2,1,0:T(2,128)S(1)} %get-tuple-element.40), channel_id=1, source_target_pairs={{1,0},{3,2},{5,4},{7,6},{9,8},{11,10},{13,12},{15,14},{17,16},{19,... | collective-permute-start | bytes 294920 | tf_op jit(solution)/shard_map/ppermute | solution.py:25
  144.1 6.5 %collective-permute-start.6 = (f32[1,3,2,4096]{3,2,1,0:T(2,128)S(1)}, f32[1,3,2,4096]{3,2,1,0:T(2,128)S(1)}, u32[]{:S(2)}, u32[]{:S(2)}) collective-permute-start(f32[1,3,2,4096]{3,2,1,0:T(2,128)S(1)} %get-tuple-element.39), channel_id=1, source_target_pairs={{0,1},{2,3},{4,5},{6,7},{8,9},{10,11},{12,13},{14,15},{16,17},{18,... | collective-permute-start | bytes 294920 | tf_op jit(solution)/shard_map/ppermute | solution.py:23
  152.1 3.7 %collective-permute-start.9 = (f32[1,3,2,4096]{3,2,1,0:T(2,128)S(1)}, f32[1,3,2,4096]{3,2,1,0:T(2,128)S(1)}, u32[]{:S(2)}, u32[]{:S(2)}) collective-permute-start(f32[1,3,2,4096]{3,2,1,0:T(2,128)S(1)} %get-tuple-element.38), channel_id=1, source_target_pairs={{1,0},{3,2},{5,4},{7,6},{9,8},{11,10},{13,12},{15,14},{17,16},{19,... | collective-permute-start | bytes 294920 | tf_op jit(solution)/shard_map/ppermute | solution.py:25
  153.6 6.5 %collective-permute-start.8 = (f32[1,3,2,4096]{3,2,1,0:T(2,128)S(1)}, f32[1,3,2,4096]{3,2,1,0:T(2,128)S(1)}, u32[]{:S(2)}, u32[]{:S(2)}) collective-permute-start(f32[1,3,2,4096]{3,2,1,0:T(2,128)S(1)} %get-tuple-element.37), channel_id=1, source_target_pairs={{0,1},{2,3},{4,5},{6,7},{8,9},{10,11},{12,13},{14,15},{16,17},{18,... | collective-permute-start | bytes 294920 | tf_op jit(solution)/shard_map/ppermute | solution.py:23
  161.6 3.7 %collective-permute-start.11 = (f32[1,3,2,4096]{3,2,1,0:T(2,128)S(1)}, f32[1,3,2,4096]{3,2,1,0:T(2,128)S(1)}, u32[]{:S(2)}, u32[]{:S(2)}) collective-permute-start(f32[1,3,2,4096]{3,2,1,0:T(2,128)S(1)} %get-tuple-element.36), channel_id=1, source_target_pairs={{1,0},{3,2},{5,4},{7,6},{9,8},{11,10},{13,12},{15,14},{17,16},{19,... | collective-permute-start | bytes 294920 | tf_op jit(solution)/shard_map/ppermute | solution.py:25
  163.1 6.5 %collective-permute-start.10 = (f32[1,3,2,4096]{3,2,1,0:T(2,128)S(1)}, f32[1,3,2,4096]{3,2,1,0:T(2,128)S(1)}, u32[]{:S(2)}, u32[]{:S(2)}) collective-permute-start(f32[1,3,2,4096]{3,2,1,0:T(2,128)S(1)} %get-tuple-element.35), channel_id=1, source_target_pairs={{0,1},{2,3},{4,5},{6,7},{8,9},{10,11},{12,13},{14,15},{16,17},{18,... | collective-permute-start | bytes 294920 | tf_op jit(solution)/shard_map/ppermute | solution.py:23
where the time goes:
time: 173 us; the launch traced here: 172 us
  local copies, waits for them, and re-layouts  46.9 us (27%)
  waiting for transfers between devices  43.1 us (25%)
  starting transfers between devices  31.2 us (18%)
  matrix products  25.8 us (15%)
  blocking collectives  15.9 us (9%)
  other arithmetic  7.95 us (5%)
    dot_general x1, matrix products, on_device(): jnp.einsum('or,poc->prc', placing, weighted, precision=lax.Precision.HIGH...  25.4 us
    unnamed x18, local copies, waits for them, and re-layouts  25 us
    ppermute x6, waiting for transfers between devices, extended(): lax.ppermute(tail, axis, [(i, (i + 1) % count) for i in range(ends)])  21.4 us
    unnamed x1, blocking collectives  15.9 us
    all_to_all x1, waiting for transfers between devices, on_device(): lax.all_to_all(chosen, 'dom', split_axis=0, concat_axis=3, tiled=True)  15.1 us
    gather x1, local copies, waits for them, and re-layouts, on_device(): jnp.take(height.reshape(local_count, band_rows * columns), position, axis=1)  11.8 us
    ppermute x6, starting transfers between devices, extended(): lax.ppermute(head, axis, [((i + 1) % count, i) for i in range(ends)])  10.9 us
    ppermute x6, starting transfers between devices, extended(): lax.ppermute(tail, axis, [(i, (i + 1) % count) for i in range(ends)])  7.93 us
  transfers between devices with their start and end apart: 14, of which 12 were waited for; matrix products, arithmetic and copies ran while one was open for 23% of the time, Pallas kernels for 0%

commit v1 on v0

v1 whole, which is shorter than its diff:
```python
import functools
import math

import jax
import jax.numpy as jnp
from jax import lax
from jax.experimental import pallas as pl
from jax.experimental.pallas import tpu as pltpu
from jax.sharding import PartitionSpec as P

STEPS = 4
BW = 8
TIME_STEP = 0.8
NUDGE_GAIN = 0.5
LENGTH_SCALE = 3.0
LANES = 128
MARGIN = 2 * STEPS


def weight(offset):
    distance = jnp.abs(offset).astype(jnp.float32)
    return jnp.where(distance <= BW, jnp.exp(-distance / LENGTH_SCALE), jnp.float32(0.0))


def cycle(
    doms, bands, rows, cols, win,
    ens, anc, depth, pos, val, out,
    hb, hw, uw, vw, dw, posb, valb, field, spread, done, relay, chosen, lineage,
    band_send, band_recv, anc_send, anc_recv, s1_send, s1_recv, s2_send, s2_recv, own_sem,
):
    me = lax.axis_index("dom")
    band = lax.axis_index("band")
    chunk = cols // doms
    blocks = cols // LANES
    wide = rows + 2 * MARGIN
    body = pl.ds(LANES, cols)

    barrier = pltpu.get_barrier_semaphore()
    for k in range(1, doms):
        pl.semaphore_signal(barrier, inc=1, device_id={"dom": lax.rem(me + k, doms)})

    has_up = band > 0
    has_down = band < bands - 1

    @pl.when(has_up)
    def _():
        pl.semaphore_signal(barrier, inc=1, device_id={"band": band - 1})

    @pl.when(has_down)
    def _():
        pl.semaphore_signal(barrier, inc=1, device_id={"band": band + 1})

    neighbours = jnp.minimum(band, 1) + jnp.minimum(bands - 1 - band, 1)
    pl.semaphore_wait(barrier, doms - 1 + neighbours)

    def band_copies(up, first=0, last=6):
        edge = pl.ds(0, MARGIN) if up else pl.ds(rows - MARGIN, MARGIN)
        halo = pl.ds(MARGIN + rows, MARGIN) if up else pl.ds(0, MARGIN)
        slot = 2 if up else 0
        way = 0 if up else 1
        target = {"band": band - 1} if up else {"band": band + 1}
        pairs = [
            (pos, posb.at[slot]),
            (val, valb.at[slot]),
            (ens.at[0, 0], hb.at[pl.ds(slot * rows, rows)]),
            (ens.at[0, 1, edge], uw.at[halo, body]),
            (ens.at[0, 2, edge], vw.at[halo, body]),
            (depth.at[edge], dw.at[halo, body]),
        ]
        return [
            pltpu.make_async_remote_copy(
                src_ref=src, dst_ref=dst,
                send_sem=band_send.at[way, i], recv_sem=band_recv.at[way, i],
                device_id=target,
            )
            for i, (src, dst) in list(enumerate(pairs))[first:last]
        ]

    @pl.when(has_up)
    def _():
        for copy in band_copies(True):
            copy.start()

    @pl.when(has_down)
    def _():
        for copy in band_copies(False):
            copy.start()

    def anc_copy(k):
        return pltpu.make_async_remote_copy(
            src_ref=anc, dst_ref=lineage.at[me],
            send_sem=anc_send.at[k], recv_sem=anc_recv.at[k],
            device_id={"dom": lax.rem(me + k, doms)},
        )

    for k in range(1, doms):
        anc_copy(k).start()
    lineage[me] = anc[...]

    own = pl.ds(MARGIN, rows)
    hb[rows : 2 * rows] = ens[0, 0]
    uw[own, body] = ens[0, 1]
    vw[own, body] = ens[0, 2]
    dw[own, body] = depth[...]
    field[0] = jnp.zeros((3 * rows, LANES), jnp.float32)
    field[blocks + 1] = jnp.zeros((3 * rows, LANES), jnp.float32)

    def place(slot, where_ref, value_ref):
        where, value = where_ref[...], value_ref[...]
        count = where.shape[1]
        group = where >> 7
        lane = where & (LANES - 1)
        high = value.astype(jnp.bfloat16).astype(jnp.float32)
        low = value - high
        hit = lax.broadcasted_iota(jnp.int32, (LANES, count), 0) == lane
        right = jnp.concatenate(
            [
                jnp.where(hit, high, 0.0).astype(jnp.bfloat16),
                jnp.where(hit, low, 0.0).astype(jnp.bfloat16),
                jnp.where(hit, 1.0, 0.0).astype(jnp.bfloat16),
            ],
            axis=0,
        )
        per = 8
        for first in range(0, blocks, per):
            index = lax.broadcasted_iota(jnp.int32, (per * rows, count), 0) + first * rows
            left = jnp.where(index == group, 1.0, 0.0).astype(jnp.bfloat16)
            placed = lax.dot_general(
                left, right, (((1,), (1,)), ((), ())), preferred_element_type=jnp.float32
            )
            for j in range(per):
                part = placed[j * rows : (j + 1) * rows]
                height = hb[slot * rows : (slot + 1) * rows, (first + j) * LANES : (first + j + 1) * LANES]
                field[first + j + 1, slot * rows : (slot + 1) * rows, :] = (
                    part[:, :LANES] + part[:, LANES : 2 * LANES] - part[:, 2 * LANES :] * height
                )

    place(1, pos, val)

    def blank(slot):
        field[:, slot * rows : (slot + 1) * rows, :] = jnp.zeros(
            (blocks + 2, rows, LANES), jnp.float32
        )
        halo = pl.ds(0, MARGIN) if slot == 0 else pl.ds(MARGIN + rows, MARGIN)
        hb[slot * rows : (slot + 1) * rows] = jnp.zeros((rows, cols), jnp.float32)
        for ref in (uw, vw, dw):
            ref[halo, body] = jnp.zeros((MARGIN, cols), jnp.float32)

    @pl.when(has_up)
    def _():
        for copy in band_copies(False, 0, 3):
            copy.wait_recv()
        place(0, posb.at[0], valb.at[0])

    @pl.when(jnp.logical_not(has_up))
    def _():
        blank(0)

    @pl.when(has_down)
    def _():
        for copy in band_copies(True, 0, 3):
            copy.wait_recv()
        place(2, posb.at[2], valb.at[2])

    @pl.when(jnp.logical_not(has_down))
    def _():
        blank(2)

    apart = lax.broadcasted_iota(jnp.int32, (LANES, LANES), 1) - lax.broadcasted_iota(
        jnp.int32, (LANES, LANES), 0
    )
    mats = [weight(apart + LANES), weight(apart), weight(apart - LANES)]
    global_row = band * rows - MARGIN + lax.broadcasted_iota(jnp.int32, (wide, 1), 0)
    inside = (global_row >= 0) & (global_row < bands * rows)
    per = 8
    for first in range(0, blocks, per):
        total = None
        for i in range(3):
            part = field[first + i : first + i + per].reshape(per * 3 * rows, LANES)
            term = jnp.dot(
                part, mats[i], precision=lax.Precision.HIGHEST, preferred_element_type=jnp.float32
            )
            total = term if total is None else total + term
        spread[first : first + per] = total.reshape(per, 3 * rows, LANES)
    base = rows - MARGIN
    for j in range(blocks):
        increment = None
        for offset in range(2 * BW + 1):
            factor = math.exp(-abs(offset - BW) / LENGTH_SCALE)
            first = base - BW + offset
            term = factor * spread[j, first : first + wide, :]
            increment = term if increment is None else increment + term
        columns = pl.ds(j * LANES, LANES)
        hw[:, (j + 1) * LANES : (j + 2) * LANES] = jnp.where(
            inside, hb[base : base + wide, columns] + NUDGE_GAIN * increment, 0.0
        )

    @pl.when(has_up)
    def _():
        for copy in band_copies(False, 3, 6):
            copy.wait_recv()

    @pl.when(has_down)
    def _():
        for copy in band_copies(True, 3, 6):
            copy.wait_recv()

    for ref in (hw, uw, vw, dw):
        ref[:, 0:LANES] = ref[:, cols : cols + LANES]
        ref[:, cols + LANES : cols + 2 * LANES] = ref[:, LANES : 2 * LANES]

    turning = 0.1 + 0.4 * ((global_row.astype(jnp.float32) + 0.5) / (bands * rows))
    turn = TIME_STEP * turning
    span = win + 2 * LANES
    windows = cols // win
    each = win // chunk

    def after(x, axis):
        return pltpu.roll(x, x.shape[axis] - 1, axis)

    def before(x, axis):
        return pltpu.roll(x, 1, axis)

    def s1_copy(k, target):
        return pltpu.make_async_remote_copy(
            src_ref=done.at[:, :, pl.ds(pl.multiple_of(target * chunk, LANES), chunk)],
            dst_ref=relay.at[me],
            send_sem=s1_send.at[k], recv_sem=s1_recv.at[k],
            device_id={"dom": target},
        )

    def window(step, carry):
        w = lax.rem(step + me, windows)
        at = pl.ds(pl.multiple_of(w * win, LANES), span)
        h, u, v, d = hw[:, at], uw[:, at], vw[:, at], dw[:, at]
        half = 0.5 * TIME_STEP
        for _ in range(STEPS):
            east, north = d * u, d * v
            diff = (after(east, 1) - before(east, 1)) + (after(north, 0) - before(north, 0))
            h = jnp.where(inside, h - half * diff, 0.0)
            new_u = u + (turn * v - half * (after(h, 1) - before(h, 1)))
            new_v = v - (turn * u + half * (after(h, 0) - before(h, 0)))
            u = jnp.where(inside, new_u, 0.0)
            v = jnp.where(inside, new_v, 0.0)
        target_cols = pl.ds(pl.multiple_of(w * win, LANES), win)
        for i, x in enumerate((h, u, v)):
            done[i, :, target_cols] = x[MARGIN : MARGIN + rows, LANES : LANES + win]
        for i in range(each):
            target = w * each + i

            @pl.when(target != me)
            def _():
                s1_copy(lax.rem(target - me + doms, doms), target).start()

        return carry

    lax.fori_loop(0, windows, window, 0)
    relay[me] = done[:, :, pl.ds(pl.multiple_of(me * chunk, LANES), chunk)]

    for k in range(1, doms):
        anc_copy(k).wait_recv()
        s1_copy(k, lax.rem(me + k, doms)).wait_recv()

    def s2_copy(k):
        target = lax.rem(me + k, doms)
        return pltpu.make_async_remote_copy(
            src_ref=chosen.at[target],
            dst_ref=out.at[0, :, :, pl.ds(pl.multiple_of(me * chunk, LANES), chunk)],
            send_sem=s2_send.at[k], recv_sem=s2_recv.at[k],
            device_id={"dom": target},
        )

    def pick(child):
        parent = lineage[child][0:1, 0:1]
        for i in range(3):
            best = relay[0, i]
            for p in range(1, doms):
                best = jnp.where(parent == p, relay[p, i], best)
            chosen[child, i] = best

    def send(k, carry):
        pick(lax.rem(me + k, doms))
        s2_copy(k).start()
        return carry

    lax.fori_loop(1, doms, send, 0)
    pick(me)
    own_copy = pltpu.make_async_copy(
        chosen.at[me],
        out.at[0, :, :, pl.ds(pl.multiple_of(me * chunk, LANES), chunk)],
        own_sem,
    )
    own_copy.start()

    @pl.when(has_up)
    def _():
        for copy in band_copies(True):
            copy.wait_send()

    @pl.when(has_down)
    def _():
        for copy in band_copies(False):
            copy.wait_send()

    for k in range(1, doms):
        anc_copy(k).wait_send()
        s1_copy(k, lax.rem(me + k, doms)).wait_send()
    own_copy.wait()
    for k in range(1, doms):
        s2_copy(k).wait()


def on_device(doms, bands, ensemble, ancestors, sea_depth, obs_rows, obs_cols, obs_values):
    _, fields, rows, cols = ensemble.shape
    count = obs_rows.shape[0]
    local_rows = obs_rows - lax.axis_index("band") * rows
    pos = (((obs_cols >> 7) * rows + local_rows) * LANES + (obs_cols & (LANES - 1)))[None, :]
    anc = jnp.broadcast_to(ancestors[:, None], (8, LANES))
    chunk = cols // doms
    blocks = cols // LANES
    win = 1024
    wide = rows + 2 * MARGIN
    f32 = jnp.float32
    dma = pltpu.SemaphoreType.DMA
    vmem = pl.BlockSpec(memory_space=pltpu.VMEM)
    return pl.pallas_call(
        functools.partial(cycle, doms, bands, rows, cols, win),
        out_shape=jax.ShapeDtypeStruct(ensemble.shape, f32),
        in_specs=[vmem] * 5,
        out_specs=pl.BlockSpec(memory_space=pl.ANY),
        scratch_shapes=[
            pltpu.VMEM((3 * rows, cols), f32),
            pltpu.VMEM((wide, cols + 2 * LANES), f32),
            pltpu.VMEM((wide, cols + 2 * LANES), f32),
            pltpu.VMEM((wide, cols + 2 * LANES), f32),
            pltpu.VMEM((wide, cols + 2 * LANES), f32),
            pltpu.VMEM((3, 1, count), jnp.int32),
            pltpu.VMEM((3, 1, count), f32),
            pltpu.VMEM((blocks + 2, 3 * rows, LANES), f32),
            pltpu.VMEM((blocks, 3 * rows, LANES), f32),
            pltpu.VMEM((fields, rows, cols), f32),
            pltpu.VMEM((doms, fields, rows, chunk), f32),
            pltpu.VMEM((doms, fields, rows, chunk), f32),
            pltpu.VMEM((doms, 8, LANES), jnp.int32),
            dma((2, 6)),
            dma((2, 6)),
            dma((doms,)),
            dma((doms,)),
            dma((doms,)),
            dma((doms,)),
            dma((doms,)),
            dma((doms,)),
            dma,
        ],
        compiler_params=pltpu.CompilerParams(
            collective_id=0, has_side_effects=True, vmem_limit_bytes=48 * 1024 * 1024
        ),
        name="cycle",
    )(ensemble, anc, sea_depth, pos, obs_values[None, :])


def solution(mesh):
    placed = (
        P("dom", None, "band", None),
        P("dom"),
        P("band", None),
        P("band"),
        P("band"),
        P("band"),
    )
    return jax.shard_map(
        functools.partial(on_device, mesh.shape["dom"], mesh.shape["band"]),
        mesh=mesh,
        in_specs=placed,
        out_specs=P("dom", None, "band", None),
        check_vma=False,
    )
```

time: 173 us -> 63.7 us (0.37)
  the two profiles are of different devices: /device:TPU:12 before, /device:TPU:27 now
where the time goes in v1:
time: 63.7 us; the launch traced here: 63.4 us
  Pallas kernels  59 us (93%)
  local copies, waits for them, and re-layouts  3.69 us (6%)
  between operations  0.71 us (1%)
    pallas_call x1, Pallas kernels, on_device(): pl.pallas_call(functools.partial(cycle, doms, bands, rows, cols, win), ou...  59 us
    unnamed x11, local copies, waits for them, and re-layouts  3.69 us

profile of v1, /device:TPU:27, one launch (start us, length us, event | category | flops | bytes accessed | tf_op | source)
XLA Modules:
  0.0 63.4 jit_solution(6014103893297634978)
XLA Ops:
  0.0 0.0 copy-start.4
  0.0 0.0 copy-start.3
  0.7 0.0 copy-done.4
  0.7 0.0 copy-done.3
  0.7 0.0 copy-start.2
  0.7 0.7 %copy-done.2 = f32[2048]{0:T(1024)S(1)} copy-done((f32[2048]{0:T(1024)S(1)}, f32[2048]{0:T(1024)}, u32[]{:S(2)}) %copy-start.2) | copy-done | bytes 8216
  1.4 0.0 copy-start
  1.4 1.1 %copy-done = f32[1,3,16,4096]{3,2,1,0:T(8,128)S(1)} copy-done((f32[1,3,16,4096]{3,2,1,0:T(8,128)S(1)}, f32[1,3,16,4096]{3,2,1,0:T(8,128)}, u32[]{:S(2)}) %copy-start) | copy-done | bytes 786456
  2.6 0.0 copy-start.1
  2.6 0.9 %copy-done.1 = f32[16,4096]{1,0:T(8,128)S(1)} copy-done((f32[16,4096]{1,0:T(8,128)S(1)}, f32[16,4096]{1,0:T(8,128)}, u32[]{:S(2)}) %copy-start.1) | copy-done | bytes 262168
  3.5 59.0 %cycle.1 = f32[1,3,16,4096]{3,2,1,0:T(8,128)S(1)} custom-call(f32[1,3,16,4096]{3,2,1,0:T(8,128)S(1)} %copy-done, s32[8,128]{1,0:T(8,128)S(1)} %broadcast_in_dim.15.anc, f32[16,4096]{1,0:T(8,128)S(1)} %copy-done.1, s32[1,2048]{1,0:T(1,128)S(1)} %bitcast.4, f32[1,2048]{1,0:T(1,128)S(1)} %bitcast.5), custom_call_target="tpu_custom_call" | custom-call | tf_op jit(solution)/shard_map/cycle/pallas_call | solution.py:326
  62.5 0.9 %copy.9 = f32[1,3,16,4096]{3,2,1,0:T(8,128)} copy(f32[1,3,16,4096]{3,2,1,0:T(8,128)S(1)} %cycle.1) | data formatting | bytes 1572864
  (2 shorter events, 0.0 us)
Async XLA Ops:
  0.0 0.7 %copy-start.4 = (s32[2048]{0:T(1024)S(1)}, s32[2048]{0:T(1024)}, u32[]{:S(2)}) copy-start(s32[2048]{0:T(1024)} %param.9) | copy-start | bytes 24580
  0.0 0.7 %copy-start.3 = (s32[2048]{0:T(1024)S(1)}, s32[2048]{0:T(1024)}, u32[]{:S(2)}) copy-start(s32[2048]{0:T(1024)} %param.10) | copy-start | bytes 24580
  0.7 0.7 %copy-start.2 = (f32[2048]{0:T(1024)S(1)}, f32[2048]{0:T(1024)}, u32[]{:S(2)}) copy-start(f32[2048]{0:T(1024)} %param.11) | copy-start | bytes 24580
  1.4 1.1 %copy-start = (f32[1,3,16,4096]{3,2,1,0:T(8,128)S(1)}, f32[1,3,16,4096]{3,2,1,0:T(8,128)}, u32[]{:S(2)}) copy-start(f32[1,3,16,4096]{3,2,1,0:T(8,128)} %ens.1) | copy-start | bytes 2359300
  2.6 0.9 %copy-start.1 = (f32[16,4096]{1,0:T(8,128)S(1)}, f32[16,4096]{1,0:T(8,128)}, u32[]{:S(2)}) copy-start(f32[16,4096]{1,0:T(8,128)} %depth.1) | copy-start | bytes 786436

commit v2 on v1

--- a/solution.py
+++ b/solution.py
@@ -26,7 +26,7 @@
     doms, bands, rows, cols, win,
     ens, anc, depth, pos, val, out,
     hb, hw, uw, vw, dw, posb, valb, field, spread, done, relay, chosen, lineage,
-    band_send, band_recv, anc_send, anc_recv, s1_send, s1_recv, s2_send, s2_recv, own_sem,
+    band_send, band_recv, anc_send, anc_recv, s1_send, s1_recv, s2_send, s2_recv, own_sem, load_sem,
 ):
     me = lax.axis_index("dom")
     band = lax.axis_index("band")
@@ -34,6 +34,21 @@
     blocks = cols // LANES
     wide = rows + 2 * MARGIN
     body = pl.ds(LANES, cols)
+
+    own = pl.ds(MARGIN, rows)
+    loads = [
+        pltpu.make_async_copy(src, dst, load_sem.at[i])
+        for i, (src, dst) in enumerate(
+            [
+                (ens.at[0, 0], hb.at[pl.ds(rows, rows)]),
+                (ens.at[0, 1], uw.at[own, body]),
+                (ens.at[0, 2], vw.at[own, body]),
+                (depth, dw.at[own, body]),
+            ]
+        )
+    ]
+    for load in loads:
+        load.start()
 
     barrier = pltpu.get_barrier_semaphore()
     for k in range(1, doms):
@@ -97,11 +112,6 @@
         anc_copy(k).start()
     lineage[me] = anc[...]
 
-    own = pl.ds(MARGIN, rows)
-    hb[rows : 2 * rows] = ens[0, 0]
-    uw[own, body] = ens[0, 1]
-    vw[own, body] = ens[0, 2]
-    dw[own, body] = depth[...]
     field[0] = jnp.zeros((3 * rows, LANES), jnp.float32)
     field[blocks + 1] = jnp.zeros((3 * rows, LANES), jnp.float32)
 
@@ -135,6 +145,7 @@
                     part[:, :LANES] + part[:, LANES : 2 * LANES] - part[:, 2 * LANES :] * height
                 )
 
+    loads[0].wait()
     place(1, pos, val)
 
     def blank(slot):
@@ -205,6 +216,9 @@
         for copy in band_copies(True, 3, 6):
             copy.wait_recv()
 
+    for load in loads[1:]:
+        load.wait()
+
     for ref in (hw, uw, vw, dw):
         ref[:, 0:LANES] = ref[:, cols : cols + LANES]
         ref[:, cols + LANES : cols + 2 * LANES] = ref[:, LANES : 2 * LANES]
@@ -278,12 +292,13 @@
                 best = jnp.where(parent == p, relay[p, i], best)
             chosen[child, i] = best
 
-    def send(k, carry):
+    def send(step, carry):
+        k = doms // 2 + ((step + 1) // 2) * (1 - 2 * (step % 2))
         pick(lax.rem(me + k, doms))
         s2_copy(k).start()
         return carry
 
-    lax.fori_loop(1, doms, send, 0)
+    lax.fori_loop(0, doms - 1, send, 0)
     pick(me)
     own_copy = pltpu.make_async_copy(
         chosen.at[me],
@@ -323,10 +338,11 @@
     f32 = jnp.float32
     dma = pltpu.SemaphoreType.DMA
     vmem = pl.BlockSpec(memory_space=pltpu.VMEM)
+    hbm = pl.BlockSpec(memory_space=pltpu.HBM)
     return pl.pallas_call(
         functools.partial(cycle, doms, bands, rows, cols, win),
         out_shape=jax.ShapeDtypeStruct(ensemble.shape, f32),
-        in_specs=[vmem] * 5,
+        in_specs=[hbm, vmem, hbm, vmem, vmem],
         out_specs=pl.BlockSpec(memory_space=pl.ANY),
         scratch_shapes=[
             pltpu.VMEM((3 * rows, cols), f32),
@@ -351,9 +367,10 @@
             dma((doms,)),
             dma((doms,)),
             dma,
+            dma((4,)),
         ],
         compiler_params=pltpu.CompilerParams(
-            collective_id=0, has_side_effects=True, vmem_limit_bytes=48 * 1024 * 1024
+            collective_id=0, has_side_effects=True, vmem_limit_bytes=127 * 512 * 1024
         ),
         name="cycle",
     )(ensemble, anc, sea_depth, pos, obs_values[None, :])

time: 63.7 us -> 69.6 us (1.093)
  the two profiles are of different devices: /device:TPU:27 before, /device:TPU:0 now
where the time goes in v2:
time: 69.6 us; the launch traced here: 69.3 us
  Pallas kernels  65.4 us (94%)
  local copies, waits for them, and re-layouts  2.66 us (4%)
    pallas_call x1, Pallas kernels, on_device(): pl.pallas_call(functools.partial(cycle, doms, bands, rows, cols, win), ou...  65.4 us
    unnamed x5, local copies, waits for them, and re-layouts  2.07 us

profile of v2, /device:TPU:0, one launch (start us, length us, event | category | flops | bytes accessed | tf_op | source)
XLA Modules:
  0.0 69.3 jit_solution(2646714005472489141)
XLA Ops:
  0.0 0.0 copy-start.1
  0.0 0.0 copy-start
  0.7 0.6 broadcast_in_dim.15.anc
  1.3 0.0 copy-done.1
  1.3 0.0 copy-done
  1.3 0.6 and_add_fusion
  1.9 65.4 %cycle.1 = f32[1,3,16,4096]{3,2,1,0:T(8,128)} custom-call(f32[1,3,16,4096]{3,2,1,0:T(8,128)} %ens.1, s32[8,128]{1,0:T(8,128)} %broadcast_in_dim.15.anc, f32[16,4096]{1,0:T(8,128)} %depth.1, s32[1,2048]{1,0:T(1,128)} %bitcast.4, f32[1,2048]{1,0:T(1,128)} %bitcast.5), custom_call_target="tpu_custom_call" | custom-call | tf_op jit(solution)/shard_map/cycle/pallas_call | solution.py:342
  67.3 2.1 %copy.9 = f32[1,3,16,4096]{3,2,1,0:T(8,128)} copy(f32[1,3,16,4096]{3,2,1,0:T(8,128)} %cycle.1) | data formatting | bytes 1572864
Async XLA Ops:
  0.0 1.3 %copy-start.1 = (s32[2048]{0:T(1024)S(1)}, s32[2048]{0:T(1024)}, u32[]{:S(2)}) copy-start(s32[2048]{0:T(1024)} %param.9) | copy-start | bytes 24580
  0.0 1.3 %copy-start = (s32[2048]{0:T(1024)S(1)}, s32[2048]{0:T(1024)}, u32[]{:S(2)}) copy-start(s32[2048]{0:T(1024)} %param.10) | copy-start | bytes 24580

commit v3 on v2

--- a/solution.py
+++ b/solution.py
@@ -64,6 +64,42 @@
     @pl.when(has_down)
     def _():
         pl.semaphore_signal(barrier, inc=1, device_id={"band": band + 1})
+
+    field[0] = jnp.zeros((3 * rows, LANES), jnp.float32)
+    field[blocks + 1] = jnp.zeros((3 * rows, LANES), jnp.float32)
+
+    def place(slot, where_ref, value_ref):
+        where, value = where_ref[...], value_ref[...]
+        count = where.shape[1]
+        group = where >> 7
+        lane = where & (LANES - 1)
+        high = value.astype(jnp.bfloat16).astype(jnp.float32)
+        low = value - high
+        hit = lax.broadcasted_iota(jnp.int32, (LANES, count), 0) == lane
+        right = jnp.concatenate(
+            [
+                jnp.where(hit, high, 0.0).astype(jnp.bfloat16),
+                jnp.where(hit, low, 0.0).astype(jnp.bfloat16),
+                jnp.where(hit, 1.0, 0.0).astype(jnp.bfloat16),
+            ],
+            axis=0,
+        )
+        per = 8
+        for first in range(0, blocks, per):
+            index = lax.broadcasted_iota(jnp.int32, (per * rows, count), 0) + first * rows
+            left = jnp.where(index == group, 1.0, 0.0).astype(jnp.bfloat16)
+            placed = lax.dot_general(
+                left, right, (((1,), (1,)), ((), ())), preferred_element_type=jnp.float32
+            )
+            for j in range(per):
+                part = placed[j * rows : (j + 1) * rows]
+                height = hb[slot * rows : (slot + 1) * rows, (first + j) * LANES : (first + j + 1) * LANES]
+                field[first + j + 1, slot * rows : (slot + 1) * rows, :] = (
+                    part[:, :LANES] + part[:, LANES : 2 * LANES] - part[:, 2 * LANES :] * height
+                )
+
+    loads[0].wait()
+    place(1, pos, val)
 
     neighbours = jnp.minimum(band, 1) + jnp.minimum(bands - 1 - band, 1)
     pl.semaphore_wait(barrier, doms - 1 + neighbours)
@@ -112,42 +148,6 @@
         anc_copy(k).start()
     lineage[me] = anc[...]
 
-    field[0] = jnp.zeros((3 * rows, LANES), jnp.float32)
-    field[blocks + 1] = jnp.zeros((3 * rows, LANES), jnp.float32)
-
-    def place(slot, where_ref, value_ref):
-        where, value = where_ref[...], value_ref[...]
-        count = where.shape[1]
-        group = where >> 7
-        lane = where & (LANES - 1)
-        high = value.astype(jnp.bfloat16).astype(jnp.float32)
-        low = value - high
-        hit = lax.broadcasted_iota(jnp.int32, (LANES, count), 0) == lane
-        right = jnp.concatenate(
-            [
-                jnp.where(hit, high, 0.0).astype(jnp.bfloat16),
-                jnp.where(hit, low, 0.0).astype(jnp.bfloat16),
-                jnp.where(hit, 1.0, 0.0).astype(jnp.bfloat16),
-            ],
-            axis=0,
-        )
-        per = 8
-        for first in range(0, blocks, per):
-            index = lax.broadcasted_iota(jnp.int32, (per * rows, count), 0) + first * rows
-            left = jnp.where(index == group, 1.0, 0.0).astype(jnp.bfloat16)
-            placed = lax.dot_general(
-                left, right, (((1,), (1,)), ((), ())), preferred_element_type=jnp.float32
-            )
-            for j in range(per):
-                part = placed[j * rows : (j + 1) * rows]
-                height = hb[slot * rows : (slot + 1) * rows, (first + j) * LANES : (first + j + 1) * LANES]
-                field[first + j + 1, slot * rows : (slot + 1) * rows, :] = (
-                    part[:, :LANES] + part[:, LANES : 2 * LANES] - part[:, 2 * LANES :] * height
-                )
-
-    loads[0].wait()
-    place(1, pos, val)
-
     def blank(slot):
         field[:, slot * rows : (slot + 1) * rows, :] = jnp.zeros(
             (blocks + 2, rows, LANES), jnp.float32
@@ -180,7 +180,12 @@
     apart = lax.broadcasted_iota(jnp.int32, (LANES, LANES), 1) - lax.broadcasted_iota(
         jnp.int32, (LANES, LANES), 0
     )
-    mats = [weight(apart + LANES), weight(apart), weight(apart - LANES)]
+
+    def halves(x):
+        high = x.astype(jnp.bfloat16)
+        return high, (x - high.astype(jnp.float32)).astype(jnp.bfloat16)
+
+    mats = [halves(weight(apart + shift)) for shift in (LANES, 0, -LANES)]
     global_row = band * rows - MARGIN + lax.broadcasted_iota(jnp.int32, (wide, 1), 0)
     inside = (global_row >= 0) & (global_row < bands * rows)
     per = 8
@@ -188,10 +193,10 @@
         total = None
         for i in range(3):
             part = field[first + i : first + i + per].reshape(per * 3 * rows, LANES)
-            term = jnp.dot(
-                part, mats[i], precision=lax.Precision.HIGHEST, preferred_element_type=jnp.float32
-            )
-            total = term if total is None else total + term
+            part_high, part_low = halves(part)
+            for x, y in ((part_high, mats[i][0]), (part_low, mats[i][0]), (part_high, mats[i][1])):
+                term = jnp.dot(x, y, preferred_element_type=jnp.float32)
+                total = term if total is None else total + term
         spread[first : first + per] = total.reshape(per, 3 * rows, LANES)
     base = rows - MARGIN
     for j in range(blocks):
@@ -292,13 +297,12 @@
                 best = jnp.where(parent == p, relay[p, i], best)
             chosen[child, i] = best
 
-    def send(step, carry):
-        k = doms // 2 + ((step + 1) // 2) * (1 - 2 * (step % 2))
+    def send(k, carry):
         pick(lax.rem(me + k, doms))
         s2_copy(k).start()
         return carry
 
-    lax.fori_loop(0, doms - 1, send, 0)
+    lax.fori_loop(1, doms, send, 0)
     pick(me)
     own_copy = pltpu.make_async_copy(
         chosen.at[me],

time: 69.6 us -> 65.3 us (0.938)
  the two profiles are of different devices: /device:TPU:0 before, /device:TPU:27 now
where the time goes in v3:
time: 65.3 us; the launch traced here: 65 us
  Pallas kernels  61 us (93%)
  local copies, waits for them, and re-layouts  2.66 us (4%)
  between operations  0.69 us (1%)
    pallas_call x1, Pallas kernels, on_device(): pl.pallas_call(functools.partial(cycle, doms, bands, rows, cols, win), ou...  61 us
    unnamed x5, local copies, waits for them, and re-layouts  2.07 us

profile of v3, /device:TPU:27, one launch (start us, length us, event | category | flops | bytes accessed | tf_op | source)
XLA Modules:
  0.0 65.0 jit_solution(11670047327434196096)
XLA Ops:
  0.0 0.0 copy-start.1
  0.0 0.0 copy-start
  0.7 0.6 broadcast_in_dim.15.anc
  1.3 0.0 copy-done.1
  1.3 0.0 copy-done
  1.3 0.6 and_add_fusion
  1.9 61.0 %cycle.1 = f32[1,3,16,4096]{3,2,1,0:T(8,128)} custom-call(f32[1,3,16,4096]{3,2,1,0:T(8,128)} %ens.1, s32[8,128]{1,0:T(8,128)} %broadcast_in_dim.15.anc, f32[16,4096]{1,0:T(8,128)} %depth.1, s32[1,2048]{1,0:T(1,128)} %bitcast.4, f32[1,2048]{1,0:T(1,128)} %bitcast.5), custom_call_target="tpu_custom_call" | custom-call | tf_op jit(solution)/shard_map/cycle/pallas_call | solution.py:346
  62.9 2.1 %copy.9 = f32[1,3,16,4096]{3,2,1,0:T(8,128)} copy(f32[1,3,16,4096]{3,2,1,0:T(8,128)} %cycle.1) | data formatting | bytes 1572864
Async XLA Ops:
  0.0 1.3 %copy-start.1 = (s32[2048]{0:T(1024)S(1)}, s32[2048]{0:T(1024)}, u32[]{:S(2)}) copy-start(s32[2048]{0:T(1024)} %param.9) | copy-start | bytes 24580
  0.0 1.3 %copy-start = (s32[2048]{0:T(1024)S(1)}, s32[2048]{0:T(1024)}, u32[]{:S(2)}) copy-start(s32[2048]{0:T(1024)} %param.10) | copy-start | bytes 24580

commit v4 on v1

--- a/solution.py
+++ b/solution.py
@@ -318,7 +318,7 @@
     anc = jnp.broadcast_to(ancestors[:, None], (8, LANES))
     chunk = cols // doms
     blocks = cols // LANES
-    win = 1024
+    win = 512
     wide = rows + 2 * MARGIN
     f32 = jnp.float32
     dma = pltpu.SemaphoreType.DMA

time: 63.7 us -> 63.4 us (level)
  Pallas kernels: 59 us -> 58.3 us
    pallas_call x1, Pallas kernels: 59 us -> 58.3 us  [on_device(): pl.pallas_call(functools.partial(cycle, doms, bands, rows, cols, win), ou...]
where the time goes in v4:
time: 63.4 us; the launch traced here: 62.7 us
  Pallas kernels  58.3 us (92%)
  local copies, waits for them, and re-layouts  3.69 us (6%)
  between operations  0.71 us (1%)
    pallas_call x1, Pallas kernels, on_device(): pl.pallas_call(functools.partial(cycle, doms, bands, rows, cols, win), ou...  58.3 us
    unnamed x11, local copies, waits for them, and re-layouts  3.69 us

profile of v4, /device:TPU:27, one launch (start us, length us, event | category | flops | bytes accessed | tf_op | source)
XLA Modules:
  0.0 62.7 jit_solution(6877141142292788816)
XLA Ops:
  0.0 0.0 copy-start.4
  0.0 0.0 copy-start.3
  0.7 0.0 copy-done.4
  0.7 0.0 copy-done.3
  0.7 0.0 copy-start.2
  0.7 0.7 %copy-done.2 = f32[2048]{0:T(1024)S(1)} copy-done((f32[2048]{0:T(1024)S(1)}, f32[2048]{0:T(1024)}, u32[]{:S(2)}) %copy-start.2) | copy-done | bytes 8216
  1.4 0.0 copy-start
  1.4 1.1 %copy-done = f32[1,3,16,4096]{3,2,1,0:T(8,128)S(1)} copy-done((f32[1,3,16,4096]{3,2,1,0:T(8,128)S(1)}, f32[1,3,16,4096]{3,2,1,0:T(8,128)}, u32[]{:S(2)}) %copy-start) | copy-done | bytes 786456
  2.6 0.0 copy-start.1
  2.6 0.9 %copy-done.1 = f32[16,4096]{1,0:T(8,128)S(1)} copy-done((f32[16,4096]{1,0:T(8,128)S(1)}, f32[16,4096]{1,0:T(8,128)}, u32[]{:S(2)}) %copy-start.1) | copy-done | bytes 262168
  3.5 58.3 %cycle.1 = f32[1,3,16,4096]{3,2,1,0:T(8,128)S(1)} custom-call(f32[1,3,16,4096]{3,2,1,0:T(8,128)S(1)} %copy-done, s32[8,128]{1,0:T(8,128)S(1)} %broadcast_in_dim.15.anc, f32[16,4096]{1,0:T(8,128)S(1)} %copy-done.1, s32[1,2048]{1,0:T(1,128)S(1)} %bitcast.4, f32[1,2048]{1,0:T(1,128)S(1)} %bitcast.5), custom_call_target="tpu_custom_call" | custom-call | tf_op jit(solution)/shard_map/cycle/pallas_call | solution.py:326
  61.8 0.9 %copy.9 = f32[1,3,16,4096]{3,2,1,0:T(8,128)} copy(f32[1,3,16,4096]{3,2,1,0:T(8,128)S(1)} %cycle.1) | data formatting | bytes 1572864
  (2 shorter events, 0.0 us)
Async XLA Ops:
  0.0 0.7 %copy-start.4 = (s32[2048]{0:T(1024)S(1)}, s32[2048]{0:T(1024)}, u32[]{:S(2)}) copy-start(s32[2048]{0:T(1024)} %param.9) | copy-start | bytes 24580
  0.0 0.7 %copy-start.3 = (s32[2048]{0:T(1024)S(1)}, s32[2048]{0:T(1024)}, u32[]{:S(2)}) copy-start(s32[2048]{0:T(1024)} %param.10) | copy-start | bytes 24580
  0.7 0.7 %copy-start.2 = (f32[2048]{0:T(1024)S(1)}, f32[2048]{0:T(1024)}, u32[]{:S(2)}) copy-start(f32[2048]{0:T(1024)} %param.11) | copy-start | bytes 24580
  1.4 1.1 %copy-start = (f32[1,3,16,4096]{3,2,1,0:T(8,128)S(1)}, f32[1,3,16,4096]{3,2,1,0:T(8,128)}, u32[]{:S(2)}) copy-start(f32[1,3,16,4096]{3,2,1,0:T(8,128)} %ens.1) | copy-start | bytes 2359300
  2.6 0.9 %copy-start.1 = (f32[16,4096]{1,0:T(8,128)S(1)}, f32[16,4096]{1,0:T(8,128)}, u32[]{:S(2)}) copy-start(f32[16,4096]{1,0:T(8,128)} %depth.1) | copy-start | bytes 786436
